TPU v7x, 32 devices: a whole 2x2x4 slice. The times are simulated.
32 devices in a mesh: row: 16 (over z, y, core), col: 2 (over x).
Axes of the slice: x: 2, y: 2, z: 4, core: 2. Of those that a mesh axis runs over, the one named last changes fastest.
Arguments:
- features: bfloat16 [16384, 128], P(('col', 'row')), may hold values from -6 to 6
- weight: bfloat16 [128, 172], replicated, may hold values from -0.5 to 0.5
- labels: int32 [16384], P(('row', 'col')), may hold values from -43 to 171
- tile_rows: int32 [16, 2, 256], P('row', 'col'), may hold values from 0 to 7, as said below
- tile_cols: int32 [16, 2, 256], P('row', 'col'), may hold values from 0 to 63
- tile_count: int32 [16, 2], P('row', 'col'), may hold values from 1 to 256, as said below
- tile_vals: bfloat16 [16, 2, 256, 128, 128], P('row', 'col'), may hold values from -0.07470703 to 0.07470703
Outputs:
- logits: float32 [16384, 172], P(('row', 'col'))
- weight_grad: float32 [128, 172], replicated
Inputs may be any that keep to these rules, and one draw needn't show every extreme that they name: `tile_rows`: within one device the used slots name distinct tiles; unused slots are ignored. `tile_count`: counts differ between devices; in every draw some device uses all 256 slots.
All inputs are finite; a program needn't handle non-finite values.
Results may differ from a plain program's by a relative error of at most 0.0029.
Values may be sent and summed in bfloat16 or wider, within the bound.
A program may use at most 128 MiB of HBM per device.

v0:
```python
import functools
import math

import jax
import jax.numpy as jnp
from jax import lax
from jax.experimental import pallas as pl
from jax.experimental.pallas import tpu as pltpu
from jax.sharding import PartitionSpec as P

F32, BF16 = jnp.float32, jnp.bfloat16
MESH = pl.DeviceIdType.MESH


def factors(n_row):
    cores = 2 if n_row % 2 == 0 else 1
    chips = n_row // cores
    la = 4 if chips % 4 == 0 else chips
    return la, chips // la, cores


def nearest(pos, size, n):
    out = 0
    for p in range(size):
        order = sorted(range(size), key=lambda s: (abs(s - p), s))
        out = out + jnp.where(pos == p, order[n], 0)
    return out


def split(x):
    hi = x.astype(BF16)
    return hi, (x - hi.astype(F32)).astype(BF16)


def dot(a, b):
    return jnp.dot(a, b, preferred_element_type=F32)


def kernel(dims, feat, weight, labels, tab, vals, logits, wgrad,
           x, tiles, acc1, acc2, out2, in1, in2, part, terms, lined, summed, w_ref, lab_ref,
           ssem, rsem, vsem, fsem, s1, r1, s2, r2, s3, r3, s4, r4, s5, r5):
    n_row, n_col, la, lb, cores, scale = dims
    slots, tile = vals.shape[0], vals.shape[1]
    bt = feat.shape[0] // tile
    ct = n_row * bt
    row, col = lax.axis_index("row"), lax.axis_index("col")
    core = row % cores
    q = (row // cores) % lb
    p = row // (cores * lb)

    def place(s, t, c):
        return (s * lb + t) * cores + c

    def when(cond, fn):
        if cond is True:
            fn()
        else:
            pl.when(cond)(fn)

    size = lb * cores * n_col
    mine = (row % (lb * cores)) * n_col + col

    def device(place_a, index):
        return (place_a * (lb * cores) + index // n_col, index % n_col)

    own = pltpu.make_async_copy(feat, x.at[row], fsem.at[0])
    own.start()
    small = [pltpu.make_async_copy(weight, w_ref, fsem.at[1]), pltpu.make_async_copy(labels, lab_ref, fsem.at[2])]
    for copy in small:
        copy.start()
    pieces = vsem.shape[0]
    fetches = [pltpu.make_async_copy(vals.at[pl.ds(n * (slots // pieces), slots // pieces)],
                                     tiles.at[pl.ds(n * (slots // pieces), slots // pieces)], vsem.at[n])
               for n in range(pieces)]
    for copy in fetches:
        copy.start()

    def loop(n, body):
        def step(k, carry):
            body(k)
            return carry
        lax.fori_loop(1, n, step, 0, unroll=n <= 8)

    barrier = pltpu.get_barrier_semaphore()
    loop(size, lambda k: pl.semaphore_signal(barrier, inc=1, device_id=device(p, (mine + k) % size), device_id_type=MESH))
    loop(la, lambda k: pl.semaphore_signal(barrier, inc=1, device_id=device((p + k) % la, mine), device_id_type=MESH))
    tiles[slots] = jnp.zeros((tile, tile), BF16)
    own.wait()
    pl.semaphore_wait(barrier, size + la - 2)

    started = []

    def send(cond, step, way, block, where):
        copy = pltpu.make_async_remote_copy(
            src_ref=x.at[block], dst_ref=x.at[block], send_sem=ssem.at[step, way], recv_sem=rsem.at[block],
            device_id={"row": where}, device_id_type=MESH)
        when(cond, copy.start)
        started.append((cond, copy))

    def arrive(block):
        pltpu.make_async_remote_copy(
            src_ref=x.at[block], dst_ref=x.at[block], send_sem=ssem.at[0, 0], recv_sem=rsem.at[block],
            device_id={"row": (row + 1) % n_row}, device_id_type=MESH).wait_recv()

    def forward(na, nb, s, t):
        block, step = place(s, t, core), na * lb + nb
        if nb == 0:
            up = p + 1 < la if na == 0 else jnp.logical_and(s < p, p + 1 < la)
            down = p > 0 if na == 0 else jnp.logical_and(s > p, p > 0)
            send(up, step, 0, block, place(p + 1, q, core))
            send(down, step, 1, block, place(p - 1, q, core))
            send(q + 1 < lb, step, 2, block, place(p, q + 1, core))
            send(q > 0, step, 3, block, place(p, q - 1, core))
        elif lb > 2:
            send(jnp.logical_and(t < q, q + 1 < lb), step, 2, block, place(p, q + 1, core))
            send(jnp.logical_and(t > q, q > 0), step, 3, block, place(p, q - 1, core))
        if cores == 2:
            send(True, step, 4, block, place(p, q, 1 - core))

    def multiply(block, acc, lo, hi, first=False):
        def body(n, carry):
            chunk = (col + n) % n_col
            lines = []
            for i in range(bt):
                at = (chunk * bt + i) * ct + block * bt
                lines.append(jnp.concatenate([tiles[tab[at + m]] for m in range(bt)], axis=1))
            y = dot(jnp.concatenate(lines, axis=0), x[block]).reshape(bt, tile, acc1.shape[2])
            rows = pl.ds(chunk * bt, bt)
            acc[rows] = y if first else acc[rows] + y
            return carry
        lax.fori_loop(lo, hi, body, 0, unroll=2 if (hi - lo) % 2 == 0 else 1)

    groups = [[(step - nb, nb) for nb in range(lb) if 0 <= step - nb < la] for step in range(la + lb - 1)]
    early = max(1, len(groups) - 2)
    exchange1, exchange2 = [], []
    tail, todo = [], []
    for g, group in enumerate(groups):
        places = [(na, nb, nearest(p, la, na), nearest(q, lb, nb)) for na, nb in group]
        for na, nb, s, t in places:
            if g > 0:
                arrive(place(s, t, core))
            forward(na, nb, s, t)
        todo += [(place(s, t, core), False) for _, _, s, t in places]
        if cores == 2:
            todo += [(place(s, t, 1 - core), True) for _, _, s, t in places]
        if g == 0 and early > 1:
            continue
        if g == min(1, early - 1):
            for copy in fetches:
                copy.wait()
        acc = acc1 if g < early else acc2
        last = g == len(groups) - 1
        for n, (block, remote) in enumerate(todo):
            if remote:
                arrive(block)
            first = g in (min(1, early - 1), early) and n == 0
            if last:
                multiply(block, acc, 1, n_col, first)
                tail.append((block, first))
            else:
                multiply(block, acc, 1, n_col + 1, first)
        todo = []
        if g == early - 1:
            for k in range(1, n_col):
                to = (col + k) % n_col
                copy = pltpu.make_async_remote_copy(
                    src_ref=acc1.at[pl.ds(to * bt, bt)], dst_ref=in1.at[k - 1], send_sem=s1.at[k - 1],
                    recv_sem=r1.at[k - 1], device_id={"col": to}, device_id_type=MESH)
                copy.start()
                exchange1.append(copy)
    for k in range(1, n_col):
        to = (col + k) % n_col
        out2[k - 1] = acc2[pl.ds(to * bt, bt)].astype(BF16)
        copy = pltpu.make_async_remote_copy(
            src_ref=out2.at[k - 1], dst_ref=in2.at[k - 1], send_sem=s2.at[k - 1],
            recv_sem=r2.at[k - 1], device_id={"col": to}, device_id_type=MESH)
        copy.start()
        exchange2.append(copy)
    for block, first in tail:
        multiply(block, acc2, n_col, n_col + 1, first)
    for copy in small:
        copy.wait()
    w = w_ref[...]
    classes, feats = w.shape
    lab = lab_ref[...]
    onehot = (lax.broadcasted_iota(jnp.int32, (classes, bt * tile), 0) == lab).astype(F32).astype(BF16)
    valid = jnp.where(lab >= 0, 1.0, 0.0).astype(F32)
    y = acc1[pl.ds(col * bt, bt)] + acc2[pl.ds(col * bt, bt)]
    for n, copy in enumerate(exchange1):
        copy.wait()
        y = y + in1[n]
    y = y.reshape(bt * tile, feats)
    hi, lo = split(y)
    picked = dot(onehot, hi) + dot(onehot, lo)
    for n, copy in enumerate(exchange2):
        copy.wait()
        late = in2[n].reshape(bt * tile, feats)
        picked = picked + dot(onehot, late)
        y = y + late.astype(F32)
    hi, lo = split(y)
    y_t = y.T
    hi_v, lo_v = split(y_t * valid)
    gram_hi, gram_lo = split(dot(hi_v, hi) + dot(hi_v, lo) + dot(lo_v, hi))
    total = dot(w, gram_hi) + dot(w, gram_lo) - picked

    per = lined.shape[1]
    owners = part.shape[0] // per
    part[pl.ds((owners - 1) * per, per)] = jnp.zeros((per, feats), F32)
    part[pl.ds(0, classes)] = total

    def rows(o):
        return pl.ds(pl.multiple_of(o * per, per), per)

    def owner(o):
        return True if owners == size else o < owners

    def term(k, to):
        return pltpu.make_async_remote_copy(
            src_ref=part.at[rows(to)], dst_ref=terms.at[k - 1], send_sem=s3.at[k - 1], recv_sem=r3.at[k - 1],
            device_id=device(p, (mine + k) % size), device_id_type=MESH)

    def across(k, source):
        return pltpu.make_async_remote_copy(
            src_ref=lined.at[source], dst_ref=lined.at[source], send_sem=s4.at[k - 1], recv_sem=r4.at[source],
            device_id=device((p + k) % la, mine), device_id_type=MESH)

    def result(k, o):
        return pltpu.make_async_remote_copy(
            src_ref=summed.at[rows(o)], dst_ref=summed.at[rows(o)], send_sem=s5.at[k - 1], recv_sem=r5.at[o],
            device_id=device(p, (mine + k) % size), device_id_type=MESH)

    def send_term(k):
        to = (mine + k) % size
        when(owner(to), lambda: term(k, to).start())
    loop(size, send_term)

    t_hi, t_lo = split(y_t)
    logits[...] = dot(w, t_hi) + dot(w, t_lo)

    def reduce():
        def add(k, value):
            term(k, 0).wait_recv()
            return value + terms[k - 1]
        lined[p] = lax.fori_loop(1, size, add, part[rows(mine)], unroll=size <= 8)
        loop(la, lambda k: across(k, p).start())
        loop(la, lambda k: across(k, (p + k) % la).wait_recv())
        value = lined[0]
        for n in range(1, la):
            value = value + lined[n]
        summed[rows(mine)] = value
        loop(size, lambda k: result(k, mine).start())
    when(owner(mine), reduce)

    def take(k):
        o = (mine + k) % size
        when(owner(o), lambda: result(k, o).wait_recv())
    loop(size, take)
    wgrad[...] = summed[pl.ds(0, classes)] * scale

    for cond, copy in started:
        when(cond, copy.wait_send)

    def sent(k):
        to = (mine + k) % size
        when(owner(to), lambda: term(k, to).wait_send())
        when(owner(mine), lambda: result(k, mine).wait_send())
    loop(size, sent)
    when(owner(mine), lambda: loop(la, lambda k: across(k, p).wait_send()))


def local(n_row, n_col, features, weight, labels, tile_rows, tile_cols, tile_count, tile_vals):
    la, lb, cores = factors(n_row)
    classes, tile, slots = weight.shape[1], tile_vals.shape[-1], tile_vals.shape[2]
    own, feat = features.shape
    bt = own // tile
    rt, ct = n_col * bt, n_row * bt
    nodes = own * n_row * n_col
    key = jnp.where(jnp.arange(slots, dtype=jnp.int32) < tile_count.reshape(()),
                    tile_rows.reshape(slots) * ct + tile_cols.reshape(slots), -1)
    match = key[:, None] == jnp.arange(rt * ct, dtype=jnp.int32)[None, :]
    table = slots + jnp.sum(jnp.where(match, jnp.arange(slots, dtype=jnp.int32)[:, None] - slots, 0), axis=0)
    dims = (n_row, n_col, la, lb, cores, 1.0 / math.sqrt(nodes))
    vmem = pl.BlockSpec(memory_space=pltpu.VMEM)
    anywhere = pl.BlockSpec(memory_space=pl.ANY)
    dma = pltpu.SemaphoreType.DMA
    peers = max(1, n_col - 1)
    size = lb * cores * n_col
    chunks = -(-classes // 8)
    per = 8 * -(-chunks // size)
    owners = -(-chunks * 8 // per)
    logits, wgrad = pl.pallas_call(
        functools.partial(kernel, dims),
        out_shape=(jax.ShapeDtypeStruct((classes, own), F32), jax.ShapeDtypeStruct((classes, feat), F32)),
        in_specs=[anywhere, anywhere, anywhere, pl.BlockSpec(memory_space=pltpu.SMEM), anywhere],
        out_specs=(vmem, vmem),
        scratch_shapes=[
            pltpu.VMEM((n_row, own, feat), BF16),
            pltpu.VMEM((slots + 1, tile, tile), BF16),
            pltpu.VMEM((rt, tile, feat), F32),
            pltpu.VMEM((rt, tile, feat), F32),
            pltpu.VMEM((peers, bt, tile, feat), BF16),
            pltpu.VMEM((peers, bt, tile, feat), F32),
            pltpu.VMEM((peers, bt, tile, feat), BF16),
            pltpu.VMEM((owners * per, feat), F32),
            pltpu.VMEM((size - 1, per, feat), F32),
            pltpu.VMEM((la, per, feat), F32),
            pltpu.VMEM((owners * per, feat), F32),
            pltpu.VMEM((classes, feat), BF16),
            pltpu.VMEM((1, own), jnp.int32),
            dma((la * lb, 5)), dma((n_row,)), dma((4,)), dma((3,)),
            dma((peers,)), dma((peers,)), dma((peers,)), dma((peers,)),
            dma((size - 1,)), dma((size - 1,)), dma((la - 1,)), dma((la,)), dma((size - 1,)), dma((owners,)),
        ],
        compiler_params=pltpu.CompilerParams(collective_id=0, has_side_effects=True, vmem_limit_bytes=60 * 2**20),
        cost_estimate=pl.CostEstimate(flops=2 * rt * ct * tile * tile * feat, bytes_accessed=slots * tile * tile * 2, transcendentals=0),
        name="aggregate",
    )(features, weight.T, labels.reshape(1, own), table, tile_vals.reshape(slots, tile, tile))
    return logits.T, wgrad.T


def solution(mesh):
    placed = (
        P(("col", "row"), None),
        P(),
        P(("row", "col")),
        P("row", "col", None),
        P("row", "col", None),
        P("row", "col"),
        P("row", "col", None, None, None),
    )
    body = functools.partial(local, mesh.shape["row"], mesh.shape["col"])
    return jax.shard_map(
        body, mesh=mesh, in_specs=placed, out_specs=(P(("row", "col"), None), P()), check_vma=False
    )
```

profile of v0, /device:TPU:0, one launch (start us, length us, event | category | flops | bytes accessed | tf_op | source)
XLA Modules:
  0.0 49.7 jit_solution(17133585080614040746)
XLA Ops:
  1.3 0.7 %multiply_add_fusion = s32[1,1,256]{2,1,0:T(1,128)S(1)} fusion(s32[1,1,256]{2,1,0:T(1,128)} %param.11, s32[1,1,256]{2,1,0:T(1,128)} %param.10), kind=kLoop, calls=%fused_computation.5 | loop fusion | flops 512 | bytes 3072 | tf_op jit(solution)/shard_map/add | solution.py:279
  2.0 0.1 select_reduce_fusion
  2.1 0.6 %broadcast_add_fusion.tab = s32[512]{0:T(512)} fusion(s32[512]{0:T(512)S(1)} %select_reduce_fusion), kind=kLoop, calls=%fused_computation.3 | loop fusion | flops 512 | bytes 4096 | tf_op jit(solution)/shard_map/add | solution.py:281
  2.7 43.7 %aggregate.1 = (f32[172,512]{1,0:T(8,128)}, f32[172,128]{1,0:T(8,128)}) custom-call(bf16[512,128]{1,0:T(8,128)(2,1)} %feat.1, bf16[172,128]{1,0:T(8,128)(2,1)} %bitcast.11, s32[1,512]{1,0:T(1,128)} %bitcast.13, s32[512]{0:T(512)} %broadcast_add_fusion.tab, bf16[256,128,128]{2,1,0:T(8,128)(2,1)} %bitcast.8), custom_call_target="tpu_custom_call" | custom-call | flops 2147483648 | bytes 8388608 | tf_op jit(solution)/shard_map/aggregate/pallas_call | solution.py:291
  46.4 1.7 %copy.12 = f32[512,172]{0,1:T(8,128)} copy(f32[512,172]{0,1:T(8,128)} %bitcast.9) | data formatting | bytes 704512
  48.1 1.5 %copy.13 = f32[128,172]{0,1:T(8,128)} copy(f32[128,172]{0,1:T(8,128)} %bitcast.10) | data formatting | bytes 176128
  (1 shorter events, 0.0 us)
where the time goes:
time: 49.9 us; the launch traced here: 49.7 us
  Pallas kernels  43.7 us (88%)
  local copies, waits for them, and re-layouts  3.28 us (7%)
  other arithmetic  1.44 us (3%)
  between operations  1.29 us (3%)
    pallas_call x1, Pallas kernels, local(): pl.pallas_call(functools.partial(kernel, dims), out_shape=(jax.ShapeDtype...  43.7 us
    unnamed x2, local copies, waits for them, and re-layouts  3.28 us

commit v1 on v0

--- a/solution.py
+++ b/solution.py
@@ -104,11 +104,10 @@
 
     def forward(na, nb, s, t):
         block, step = place(s, t, core), na * lb + nb
+        if na == 0 and nb == 0:
+            for n in range(1, la):
+                send(True, step, 4 + n, block, place(nearest(p, la, n), q, core))
         if nb == 0:
-            up = p + 1 < la if na == 0 else jnp.logical_and(s < p, p + 1 < la)
-            down = p > 0 if na == 0 else jnp.logical_and(s > p, p > 0)
-            send(up, step, 0, block, place(p + 1, q, core))
-            send(down, step, 1, block, place(p - 1, q, core))
             send(q + 1 < lb, step, 2, block, place(p, q + 1, core))
             send(q > 0, step, 3, block, place(p, q - 1, core))
         elif lb > 2:
@@ -120,46 +119,58 @@
     def multiply(block, acc, lo, hi, first=False):
         def body(n, carry):
             chunk = (col + n) % n_col
-            lines = []
-            for i in range(bt):
-                at = (chunk * bt + i) * ct + block * bt
-                lines.append(jnp.concatenate([tiles[tab[at + m]] for m in range(bt)], axis=1))
-            y = dot(jnp.concatenate(lines, axis=0), x[block]).reshape(bt, tile, acc1.shape[2])
-            rows = pl.ds(chunk * bt, bt)
-            acc[rows] = y if first else acc[rows] + y
+            half = max(1, bt // 2)
+            for i in range(0, bt, half):
+                lines = []
+                for m in range(i, i + half):
+                    at = (chunk * bt + m) * ct + block * bt
+                    lines.append(jnp.concatenate([tiles[tab[at + j]] for j in range(bt)], axis=1))
+                y = dot(jnp.concatenate(lines, axis=0), x[block]).reshape(half, tile, acc1.shape[2])
+                rows = pl.ds(chunk * bt + i, half)
+                acc[rows] = y if first else acc[rows] + y
             return carry
         lax.fori_loop(lo, hi, body, 0, unroll=2 if (hi - lo) % 2 == 0 else 1)
 
     groups = [[(step - nb, nb) for nb in range(lb) if 0 <= step - nb < la] for step in range(la + lb - 1)]
-    early = max(1, len(groups) - 2)
+    early = max(1, len(groups) - 3)
     exchange1, exchange2 = [], []
-    tail, todo = [], []
-    for g, group in enumerate(groups):
-        places = [(na, nb, nearest(p, la, na), nearest(q, lb, nb)) for na, nb in group]
-        for na, nb, s, t in places:
+    tail, begun = [], []
+    where = [[(na, nb, nearest(p, la, na), nearest(q, lb, nb)) for na, nb in group] for group in groups]
+
+    def pass_on(g):
+        for na, nb, s, t in where[g]:
             if g > 0:
                 arrive(place(s, t, core))
             forward(na, nb, s, t)
-        todo += [(place(s, t, core), False) for _, _, s, t in places]
-        if cores == 2:
-            todo += [(place(s, t, 1 - core), True) for _, _, s, t in places]
-        if g == 0 and early > 1:
-            continue
-        if g == min(1, early - 1):
-            for copy in fetches:
-                copy.wait()
+
+    def compute(g, sibling):
         acc = acc1 if g < early else acc2
-        last = g == len(groups) - 1
-        for n, (block, remote) in enumerate(todo):
-            if remote:
+        for _, _, s, t in where[g]:
+            block = place(s, t, 1 - core if sibling else core)
+            if sibling:
                 arrive(block)
-            first = g in (min(1, early - 1), early) and n == 0
-            if last:
+            first = not any(acc is other for other in begun)
+            begun.append(acc)
+            if g == len(groups) - 1:
                 multiply(block, acc, 1, n_col, first)
                 tail.append((block, first))
             else:
                 multiply(block, acc, 1, n_col + 1, first)
-        todo = []
+
+    pass_on(0)
+    for g in range(len(groups)):
+        if g == 0 and len(groups) > 1:
+            pass_on(1)
+        if g == 0:
+            for copy in fetches:
+                copy.wait()
+        compute(g, False)
+        if 0 < g < len(groups) - 2:
+            pass_on(g + 1)
+        if cores == 2:
+            compute(g, True)
+        if 0 < g == len(groups) - 2:
+            pass_on(g + 1)
         if g == early - 1:
             for k in range(1, n_col):
                 to = (col + k) % n_col
@@ -307,11 +318,11 @@
             pltpu.VMEM((owners * per, feat), F32),
             pltpu.VMEM((classes, feat), BF16),
             pltpu.VMEM((1, own), jnp.int32),
-            dma((la * lb, 5)), dma((n_row,)), dma((4,)), dma((3,)),
+            dma((la * lb, 4 + la)), dma((n_row,)), dma((4,)), dma((3,)),
             dma((peers,)), dma((peers,)), dma((peers,)), dma((peers,)),
             dma((size - 1,)), dma((size - 1,)), dma((la - 1,)), dma((la,)), dma((size - 1,)), dma((owners,)),
         ],
-        compiler_params=pltpu.CompilerParams(collective_id=0, has_side_effects=True, vmem_limit_bytes=60 * 2**20),
+        compiler_params=pltpu.CompilerParams(collective_id=0, has_side_effects=True, vmem_limit_bytes=48 * 2**20),
         cost_estimate=pl.CostEstimate(flops=2 * rt * ct * tile * tile * feat, bytes_accessed=slots * tile * tile * 2, transcendentals=0),
         name="aggregate",
     )(features, weight.T, labels.reshape(1, own), table, tile_vals.reshape(slots, tile, tile))

time: 49.9 us -> 51 us (1.022)
  Pallas kernels: 43.7 us -> 44.8 us
  other arithmetic: 1.44 us -> 0.86 us
    pallas_call x1, Pallas kernels: 43.7 us -> 44.8 us  [local(): pl.pallas_call(functools.partial(kernel, dims), out_shape=(jax.ShapeDtype...]
    add x1, other arithmetic: 0.59 us -> 0.01 us  [local(): slots + jnp.sum(jnp.where(match, jnp.arange(slots, dtype=jnp.int32)[:, No...]
    unnamed x2 -> x8, local copies, waits for them, and re-layouts: 3.28 us -> 3.74 us
where the time goes in v1:
time: 51 us; the launch traced here: 50.8 us
  Pallas kernels  44.8 us (88%)
  local copies, waits for them, and re-layouts  3.74 us (7%)
  between operations  1.3 us (3%)
  other arithmetic  0.86 us (2%)
    pallas_call x1, Pallas kernels, local(): pl.pallas_call(functools.partial(kernel, dims), out_shape=(jax.ShapeDtype...  44.8 us
    unnamed x8, local copies, waits for them, and re-layouts  3.74 us

profile of v1, /device:TPU:0, one launch (start us, length us, event | category | flops | bytes accessed | tf_op | source)
XLA Modules:
  0.0 50.8 jit_solution(15835816179370482012)
XLA Ops:
  1.3 0.7 %multiply_add_fusion = s32[1,1,256]{2,1,0:T(1,128)S(1)} fusion(s32[1,1,256]{2,1,0:T(1,128)} %param.11, s32[1,1,256]{2,1,0:T(1,128)} %param.10), kind=kLoop, calls=%fused_computation.5 | loop fusion | flops 512 | bytes 3072 | tf_op jit(solution)/shard_map/add | solution.py:290
  2.0 0.1 select_reduce_fusion
  2.1 0.0 copy-start
  2.2 0.9 %copy-done = bf16[512,128]{1,0:T(8,128)(2,1)S(1)} copy-done((bf16[512,128]{1,0:T(8,128)(2,1)S(1)}, bf16[512,128]{1,0:T(8,128)(2,1)}, u32[]{:S(2)}) %copy-start) | copy-done | bytes 131096
  3.1 0.0 copy-start.1
  3.1 0.8 %copy-done.1 = bf16[128,172]{0,1:T(8,128)(2,1)S(1)} copy-done((bf16[128,172]{0,1:T(8,128)(2,1)S(1)}, bf16[128,172]{0,1:T(8,128)(2,1)}, u32[]{:S(2)}) %copy-start.1) | copy-done | bytes 44056
  3.8 0.0 copy-start.2
  3.8 0.7 %copy-done.2 = s32[512]{0:T(512)S(1)} copy-done((s32[512]{0:T(512)S(1)}, s32[512]{0:T(512)}, u32[]{:S(2)}) %copy-start.2) | copy-done | bytes 2072
  4.5 44.8 %aggregate.1 = (f32[172,512]{1,0:T(8,128)S(1)}, f32[172,128]{1,0:T(8,128)S(1)}) custom-call(bf16[512,128]{1,0:T(8,128)(2,1)S(1)} %copy-done, bf16[172,128]{1,0:T(8,128)(2,1)S(1)} %bitcast.10, s32[1,512]{1,0:T(1,128)S(1)} %bitcast.11, s32[512]{0:T(512)S(1)} %broadcast_add_fusion.tab, bf16[256,128,128]{2,1,0:T(8,128)(2,1)} %bitcast.12), custom_call_target="tpu_custom_call" | custom-call | flops 2147483648 | bytes 8388608 | tf_op jit(solution)/shard_map/aggregate/pallas_call | solution.py:302
  49.4 0.7 %copy.12 = f32[512,172]{0,1:T(8,128)} copy(f32[512,172]{0,1:T(8,128)S(1)} %bitcast.8) | data formatting | bytes 704512
  50.1 0.6 %copy.13 = f32[128,172]{0,1:T(8,128)} copy(f32[128,172]{0,1:T(8,128)S(1)} %bitcast.9) | data formatting | bytes 176128
  (2 shorter events, 0.0 us)
Async XLA Ops:
  2.1 0.9 %copy-start = (bf16[512,128]{1,0:T(8,128)(2,1)S(1)}, bf16[512,128]{1,0:T(8,128)(2,1)}, u32[]{:S(2)}) copy-start(bf16[512,128]{1,0:T(8,128)(2,1)} %feat.1) | copy-start | bytes 393220
  3.1 0.8 %copy-start.1 = (bf16[128,172]{0,1:T(8,128)(2,1)S(1)}, bf16[128,172]{0,1:T(8,128)(2,1)}, u32[]{:S(2)}) copy-start(bf16[128,172]{0,1:T(8,128)(2,1)} %param.8) | copy-start | bytes 132100
  3.8 0.7 %copy-start.2 = (s32[512]{0:T(512)S(1)}, s32[512]{0:T(512)}, u32[]{:S(2)}) copy-start(s32[512]{0:T(512)} %param.9) | copy-start | bytes 6148

commit v2 on v0

--- a/solution.py
+++ b/solution.py
@@ -84,6 +84,8 @@
     barrier = pltpu.get_barrier_semaphore()
     loop(size, lambda k: pl.semaphore_signal(barrier, inc=1, device_id=device(p, (mine + k) % size), device_id_type=MESH))
     loop(la, lambda k: pl.semaphore_signal(barrier, inc=1, device_id=device((p + k) % la, mine), device_id_type=MESH))
+    acc1[...] = jnp.zeros_like(acc1)
+    acc2[...] = jnp.zeros_like(acc2)
     tiles[slots] = jnp.zeros((tile, tile), BF16)
     own.wait()
     pl.semaphore_wait(barrier, size + la - 2)
@@ -117,18 +119,24 @@
         if cores == 2:
             send(True, step, 4, block, place(p, q, 1 - core))
 
-    def multiply(block, acc, lo, hi, first=False):
-        def body(n, carry):
-            chunk = (col + n) % n_col
-            lines = []
-            for i in range(bt):
-                at = (chunk * bt + i) * ct + block * bt
-                lines.append(jnp.concatenate([tiles[tab[at + m]] for m in range(bt)], axis=1))
-            y = dot(jnp.concatenate(lines, axis=0), x[block]).reshape(bt, tile, acc1.shape[2])
-            rows = pl.ds(chunk * bt, bt)
-            acc[rows] = y if first else acc[rows] + y
-            return carry
-        lax.fori_loop(lo, hi, body, 0, unroll=2 if (hi - lo) % 2 == 0 else 1)
+    def multiply(blocks, passed, acc, lo, hi):
+        def body(e, carry):
+            block = 0
+            for n, b in enumerate(blocks):
+                block = block + jnp.where(e == n, b, 0)
+            pl.when(e >= passed)(lambda: arrive(block))
+
+            def rows(n, carry):
+                chunk = (col + n) % n_col
+                lines = []
+                for i in range(bt):
+                    at = (chunk * bt + i) * ct + block * bt
+                    lines.append(jnp.concatenate([tiles[tab[at + m]] for m in range(bt)], axis=1))
+                y = dot(jnp.concatenate(lines, axis=0), x[block]).reshape(bt, tile, acc1.shape[2])
+                acc[pl.ds(chunk * bt, bt)] += y
+                return carry
+            return lax.fori_loop(lo, hi, rows, carry)
+        lax.fori_loop(0, len(blocks), body, 0)
 
     groups = [[(step - nb, nb) for nb in range(lb) if 0 <= step - nb < la] for step in range(la + lb - 1)]
     early = max(1, len(groups) - 2)
@@ -150,15 +158,12 @@
                 copy.wait()
         acc = acc1 if g < early else acc2
         last = g == len(groups) - 1
-        for n, (block, remote) in enumerate(todo):
-            if remote:
-                arrive(block)
-            first = g in (min(1, early - 1), early) and n == 0
-            if last:
-                multiply(block, acc, 1, n_col, first)
-                tail.append((block, first))
-            else:
-                multiply(block, acc, 1, n_col + 1, first)
+        todo.sort(key=lambda entry: entry[1])
+        blocks = [block for block, _ in todo]
+        passed = sum(not remote for _, remote in todo)
+        multiply(blocks, passed, acc, 1, n_col if last else n_col + 1)
+        if last:
+            tail = blocks
         todo = []
         if g == early - 1:
             for k in range(1, n_col):
@@ -176,8 +181,7 @@
             recv_sem=r2.at[k - 1], device_id={"col": to}, device_id_type=MESH)
         copy.start()
         exchange2.append(copy)
-    for block, first in tail:
-        multiply(block, acc2, n_col, n_col + 1, first)
+    multiply(tail, len(tail), acc2, n_col, n_col + 1)
     for copy in small:
         copy.wait()
     w = w_ref[...]

time: 49.9 us -> 50.4 us (1.010)
    pallas_call x1, Pallas kernels: 43.7 us -> 44.2 us  [local(): pl.pallas_call(functools.partial(kernel, dims), out_shape=(jax.ShapeDtype...]
where the time goes in v2:
time: 50.4 us; the launch traced here: 50.2 us
  Pallas kernels  44.2 us (88%)
  local copies, waits for them, and re-layouts  3.28 us (7%)
  other arithmetic  1.44 us (3%)
  between operations  1.29 us (3%)
    pallas_call x1, Pallas kernels, local(): pl.pallas_call(functools.partial(kernel, dims), out_shape=(jax.ShapeDtype...  44.2 us
    unnamed x2, local copies, waits for them, and re-layouts  3.28 us

profile of v2, /device:TPU:0, one launch (start us, length us, event | category | flops | bytes accessed | tf_op | source)
XLA Modules:
  0.0 50.2 jit_solution(11320090424382841235)
XLA Ops:
  1.3 0.7 %multiply_add_fusion = s32[1,1,256]{2,1,0:T(1,128)S(1)} fusion(s32[1,1,256]{2,1,0:T(1,128)} %param.11, s32[1,1,256]{2,1,0:T(1,128)} %param.10), kind=kLoop, calls=%fused_computation.5 | loop fusion | flops 512 | bytes 3072 | tf_op jit(solution)/shard_map/add | solution.py:283
  2.0 0.1 select_reduce_fusion
  2.1 0.6 %broadcast_add_fusion.tab = s32[512]{0:T(512)} fusion(s32[512]{0:T(512)S(1)} %select_reduce_fusion), kind=kLoop, calls=%fused_computation.3 | loop fusion | flops 512 | bytes 4096 | tf_op jit(solution)/shard_map/add | solution.py:285
  2.7 44.2 %aggregate.1 = (f32[172,512]{1,0:T(8,128)}, f32[172,128]{1,0:T(8,128)}) custom-call(bf16[512,128]{1,0:T(8,128)(2,1)} %feat.1, bf16[172,128]{1,0:T(8,128)(2,1)} %bitcast.11, s32[1,512]{1,0:T(1,128)} %bitcast.13, s32[512]{0:T(512)} %broadcast_add_fusion.tab, bf16[256,128,128]{2,1,0:T(8,128)(2,1)} %bitcast.8), custom_call_target="tpu_custom_call" | custom-call | flops 2147483648 | bytes 8388608 | tf_op jit(solution)/shard_map/aggregate/pallas_call | solution.py:295
  46.9 1.7 %copy.12 = f32[512,172]{0,1:T(8,128)} copy(f32[512,172]{0,1:T(8,128)} %bitcast.9) | data formatting | bytes 704512
  48.7 1.5 %copy.13 = f32[128,172]{0,1:T(8,128)} copy(f32[128,172]{0,1:T(8,128)} %bitcast.10) | data formatting | bytes 176128
  (1 shorter events, 0.0 us)

commit v3 on v0

--- a/solution.py
+++ b/solution.py
@@ -72,8 +72,6 @@
     fetches = [pltpu.make_async_copy(vals.at[pl.ds(n * (slots // pieces), slots // pieces)],
                                      tiles.at[pl.ds(n * (slots // pieces), slots // pieces)], vsem.at[n])
                for n in range(pieces)]
-    for copy in fetches:
-        copy.start()
 
     def loop(n, body):
         def step(k, carry):
@@ -140,6 +138,9 @@
             if g > 0:
                 arrive(place(s, t, core))
             forward(na, nb, s, t)
+        if g == 0:
+            for copy in fetches:
+                copy.start()
         todo += [(place(s, t, core), False) for _, _, s, t in places]
         if cores == 2:
             todo += [(place(s, t, 1 - core), True) for _, _, s, t in places]

time: 49.9 us -> 49.9 us (level)
  no operation moved by 1% of the time
where the time goes in v3:
time: 49.9 us; the launch traced here: 49.7 us
  Pallas kernels  43.7 us (88%)
  local copies, waits for them, and re-layouts  3.28 us (7%)
  other arithmetic  1.44 us (3%)
  between operations  1.29 us (3%)
    pallas_call x1, Pallas kernels, local(): pl.pallas_call(functools.partial(kernel, dims), out_shape=(jax.ShapeDtype...  43.7 us
    unnamed x2, local copies, waits for them, and re-layouts  3.28 us

profile of v3, /device:TPU:0, one launch (start us, length us, event | category | flops | bytes accessed | tf_op | source)
XLA Modules:
  0.0 49.7 jit_solution(12144273943769899646)
XLA Ops:
  1.3 0.7 %multiply_add_fusion = s32[1,1,256]{2,1,0:T(1,128)S(1)} fusion(s32[1,1,256]{2,1,0:T(1,128)} %param.11, s32[1,1,256]{2,1,0:T(1,128)} %param.10), kind=kLoop, calls=%fused_computation.5 | loop fusion | flops 512 | bytes 3072 | tf_op jit(solution)/shard_map/add | solution.py:280
  2.0 0.1 select_reduce_fusion
  2.1 0.6 %broadcast_add_fusion.tab = s32[512]{0:T(512)} fusion(s32[512]{0:T(512)S(1)} %select_reduce_fusion), kind=kLoop, calls=%fused_computation.3 | loop fusion | flops 512 | bytes 4096 | tf_op jit(solution)/shard_map/add | solution.py:282
  2.7 43.7 %aggregate.1 = (f32[172,512]{1,0:T(8,128)}, f32[172,128]{1,0:T(8,128)}) custom-call(bf16[512,128]{1,0:T(8,128)(2,1)} %feat.1, bf16[172,128]{1,0:T(8,128)(2,1)} %bitcast.11, s32[1,512]{1,0:T(1,128)} %bitcast.13, s32[512]{0:T(512)} %broadcast_add_fusion.tab, bf16[256,128,128]{2,1,0:T(8,128)(2,1)} %bitcast.8), custom_call_target="tpu_custom_call" | custom-call | flops 2147483648 | bytes 8388608 | tf_op jit(solution)/shard_map/aggregate/pallas_call | solution.py:292
  46.4 1.7 %copy.12 = f32[512,172]{0,1:T(8,128)} copy(f32[512,172]{0,1:T(8,128)} %bitcast.9) | data formatting | bytes 704512
  48.1 1.5 %copy.13 = f32[128,172]{0,1:T(8,128)} copy(f32[128,172]{0,1:T(8,128)} %bitcast.10) | data formatting | bytes 176128
  (1 shorter events, 0.0 us)
